TPU v7x, 32 devices: a whole 2x2x4 slice. The times are simulated.
32 devices in a mesh: row: 16 (over z, y, x), col: 2 (over core).
Axes of the slice: x: 2, y: 2, z: 4, core: 2. Of those that a mesh axis runs over, the one named last changes fastest.
Arguments:
- top_inverse: float32 [2, 1024, 1024], P(None, 'row', 'col'), may hold values from -6 to 6, as said below
- blocks_upper: int32 [2, 2], replicated, may hold values from 0 to 3, as said below
- factor_upper: float32 [2, 2, 512, 4096], P(None, None, 'row', 'col'), may hold values from -0.1875 to 0.1875
- diagonal_upper: float32 [2, 2, 4096, 4096], P(None, None, 'row', 'col'), may hold values from -6 to 6, as said below
- parents_lower: int32 [3], replicated, may hold values from 0 to 1
- blocks_lower: int32 [3, 2], replicated, may hold values from 0 to 15, as said below
- factor_lower: float32 [3, 2, 512, 4096], P(None, None, 'row', 'col'), may hold values from -0.1875 to 0.1875
- diagonal_lower: float32 [3, 2, 4096, 4096], P(None, None, 'row', 'col'), may hold values from -6 to 6, as said below
Outputs:
- coupling_inverse_upper: float32 [2, 2, 4096, 512], P(None, None, 'row')
- block_inverse_upper: float32 [2, 2, 4096, 4096], P(None, None, 'row', 'col')
- coupling_inverse_lower: float32 [3, 2, 4096, 512], P(None, None, 'row')
- block_inverse_lower: float32 [3, 2, 4096, 4096], P(None, None, 'row', 'col')
Inputs may be any that keep to these rules, and one draw needn't show every extreme that they name: `top_inverse`: equal to its own transpose (no conjugation) in both parts. `diagonal_upper`: each matrix equals its own transpose (no conjugation) in both parts. `diagonal_lower`: each matrix equals its own transpose (no conjugation) in both parts. `blocks_upper`: each row names 2 different blocks. `blocks_lower`: each row names 2 different blocks.
All inputs are finite; a program needn't handle non-finite values.
Results may differ from a plain program's by a relative error of at most 0.00011.
Values sent between devices are 32-bit elements; how exact they have to be, the bound alone decides.
A program may use at most 256 MiB of HBM per device.

v0:
```python
import jax
import jax.numpy as jnp
from jax import lax
from jax.sharding import PartitionSpec as P

BS = 256
KB = 16
NB = 2
NTB = 4
UPPER = 2


def from_root(block, axis, source):
    block = jnp.where(lax.axis_index(axis) == source, block, jnp.zeros_like(block))
    return lax.psum(block, axis)


def complex_product(first_side, second_side, pattern):
    pieces_all = jnp.einsum(
        pattern,
        first_side,
        second_side,
        precision=lax.Precision.HIGHEST,
        preferred_element_type=jnp.float32,
    )
    real_part = pieces_all[:, 0, 0] - pieces_all[:, 1, 1]
    imag_part = pieces_all[:, 0, 1] + pieces_all[:, 1, 0]
    return jnp.stack([real_part, imag_part], axis=1)


def pick_blocks(stacked, blocks, blocks_total, rows_within, cols_within):
    batch_size = stacked.shape[0]
    tiled_view = stacked.reshape(
        batch_size, 2, rows_within, blocks_total, cols_within, blocks_total
    )

    def pick_single(matrix, chosen):
        matrix = jnp.take(matrix, chosen, axis=2)
        matrix = jnp.take(matrix, chosen, axis=4)
        return matrix.reshape(2, rows_within * NB, cols_within * NB)

    return jax.vmap(pick_single)(tiled_view, blocks)


def supernode_level(chosen, factor_rows, diag_block, slice_start, root_col):
    gathered_factor = lax.all_gather(factor_rows, "row", axis=2, tiled=True)
    factor_columns = lax.dynamic_slice_in_dim(gathered_factor, slice_start, diag_block.shape[2], 3)
    factor_slice = from_root(factor_columns, "col", root_col)
    zeroes = jnp.zeros(
        factor_slice.shape[:2] + (factor_slice.shape[3], chosen.shape[3]), jnp.float32
    )
    factor_part = factor_slice
    coupled_part = zeroes - complex_product(
        factor_part, lax.all_gather(chosen, "row", axis=2, tiled=True), "bikm,bjkn->bijmn"
    )
    incoming = lax.all_gather(coupled_part, "col", axis=3, tiled=True)
    block_total = diag_block
    factor_part = gathered_factor
    block_total = block_total - complex_product(incoming, factor_part, "bimk,bjkn->bijmn")
    gathered = incoming
    block_total, gathered = (block_total, gathered)
    return (gathered, block_total)


def shards(
    top_inverse,
    blocks_upper,
    factor_upper,
    diagonal_upper,
    parents_lower,
    blocks_lower,
    factor_lower,
    diagonal_lower,
):
    row_devices = lax.axis_size("row")
    col_devices = lax.axis_size("col")
    rows_within = BS // row_devices
    cols_within = BS // col_devices
    ratio_axes = row_devices // col_devices
    my_row = lax.axis_index("row")
    root_col = my_row // ratio_axes
    slice_start = my_row % ratio_axes * rows_within * KB
    upper_spans = (0, UPPER)
    first_index, last_index = upper_spans
    width_now = last_index - first_index
    source = jnp.broadcast_to(top_inverse, (width_now,) + top_inverse.shape)
    chosen = pick_blocks(source, blocks_upper, NTB, rows_within, cols_within)
    coupling_out, block_out = supernode_level(
        chosen, factor_upper, diagonal_upper, slice_start, root_col
    )
    upper_coupling = coupling_out
    upper_blocks = block_out
    source = jnp.take(upper_blocks, parents_lower, axis=0)
    chosen = pick_blocks(source, blocks_lower, KB, rows_within, cols_within)
    coupling_out, block_out = supernode_level(
        chosen, factor_lower, diagonal_lower, slice_start, root_col
    )
    return (upper_coupling, upper_blocks, coupling_out, block_out)


def solution(mesh):
    placed = (
        P(None, "row", "col"),
        P(),
        P(None, None, "row", "col"),
        P(None, None, "row", "col"),
        P(),
        P(),
        P(None, None, "row", "col"),
        P(None, None, "row", "col"),
    )
    return jax.shard_map(
        shards,
        mesh=mesh,
        in_specs=placed,
        out_specs=(
            P(None, None, "row", None),
            P(None, None, "row", "col"),
            P(None, None, "row", None),
            P(None, None, "row", "col"),
        ),
        check_vma=False,
    )
```

profile of v0, /device:TPU:0, one launch (start us, length us, event | category | flops | bytes accessed | tf_op | source)
XLA Modules:
  0.0 991.4 jit_solution(4863785366521610066)
XLA Ops:
  7.2 0.7 all-gather.9.cloned.1.call-update
  7.9 0.7 all-gather.15.cloned.1.call-update
  8.6 0.0 all-gather.7.cloned.1.call-start
  8.7 10.8 %broadcast_in_dim.86 = f32[2,16,4,128,4]{4,3,2,1,0:T(8,128)} reshape(f32[2,64,512]{2,1,0:T(8,128)} %param.8) | data formatting | bytes 524288 | tf_op jit(solution)/shard_map/broadcast_in_dim | solution.py:86
  19.5 5.6 copy.76
  25.1 0.1 reshape.177
  25.3 0.6 gather_fusion
  25.9 0.1 fusion.40
  26.0 0.6 gather_fusion.1
  26.5 4.6 copy.78
  31.2 7.0 gather.28
  38.2 0.1 broadcast_in_dim.83
  38.3 0.7 broadcast_select_fusion.2
  39.0 0.0 all-reduce.3.cloned.1.call-start
  39.1 165.9 %all-gather.9.cloned.1.call-done = f32[2,2,512,2048]{3,2,1,0:T(8,128)} async-done(((f32[2,2,32,2048]{3,2,1,0:T(8,128)}), f32[2,2,512,2048]{3,2,1,0:T(8,128)}) %all-gather.9.cloned.1.call-update) | async-done | bytes 16777232 | tf_op jit(solution)/shard_map/all_gather | solution.py:46
  204.9 3.1 dynamic-slice_select_fusion.1
  208.0 268.8 %all-gather.15.cloned.1.call-done = f32[3,2,512,2048]{3,2,1,0:T(8,128)} async-done(((f32[3,2,32,2048]{3,2,1,0:T(8,128)}), f32[3,2,512,2048]{3,2,1,0:T(8,128)}) %all-gather.15.cloned.1.call-update) | async-done | bytes 25165840 | tf_op jit(solution)/shard_map/all_gather | solution.py:46
  476.8 3.9 dynamic-slice_select_fusion
  480.7 0.0 all-gather.11.cloned.1.call-start
  480.8 58.5 %all-gather.7.cloned.1.call-done = f32[2,2,512,256]{3,2,1,0:T(8,128)} async-done(((f32[2,2,32,256]{3,2,1,0:T(8,128)}), f32[2,2,512,256]{3,2,1,0:T(8,128)}) %all-gather.7.cloned.1.call-update) | async-done | bytes 2097168 | tf_op jit(solution)/shard_map/all_gather | solution.py:54
  539.2 32.0 %all-reduce.3.cloned.1.call-done = (f32[2,2,512,256]{3,2,1,0:T(8,128)}, f32[3,2,512,256]{3,2,1,0:T(8,128)}) async-done(((f32[2,2,512,256]{3,2,1,0:T(8,128)}, f32[3,2,512,256]{3,2,1,0:T(8,128)}), (f32[2,2,512,256]{3,2,1,0:T(8,128)}, f32[3,2,512,256]{3,2,1,0:T(8,128)})) %all-reduce.3.cloned.1.call-update) | async-done | bytes 5242896 | tf_op jit(solution)/shard_map/psum | solution.py:15
  571.2 5.7 fusion.29
  576.9 0.1 fusion.37
  577.0 0.1 fusion.39
  577.1 1.1 maximum_subtract_fusion.3
  578.2 0.5 all-gather.13.cloned.1.call-start
  578.7 0.1 copy.87
  578.8 0.1 reshape.189
  578.9 0.1 copy.85
  579.0 0.7 broadcast_in_dim.94
  579.8 10.3 %all-gather.11.cloned.1.call-done = f32[2,2,256,512]{2,3,0,1:T(8,128)} async-done(((f32[2,2,256,256]{2,3,0,1:T(8,128)}), f32[2,2,256,512]{2,3,0,1:T(8,128)}) %all-gather.11.cloned.1.call-update) | async-done | bytes 2097168 | tf_op jit(solution)/shard_map/all_gather | solution.py:56
  590.0 32.2 %fusion.7 = f32[2,2,2,256,2048]{4,3,2,1,0:T(8,128)S(1)} fusion(f32[2,2,512,2048]{3,2,1,0:T(8,128)} %all-gather.9.cloned.1.call-done, f32[2,2,256,512]{2,3,0,1:T(8,128)} %all-gather.11.cloned.1.call-done), kind=kOutput, calls=%fused_computation.15 | convolution fusion | flops 25769803776 | bytes 35651584 | tf_op jit(solution)/shard_map/bimk,bjkn->bijmn/dot_general | solution.py:19
  622.3 0.8 fusion.13
  623.1 0.8 fusion.15
  623.8 4.4 maximum_subtract_fusion.1
  628.3 4.5 fusion.41
  632.8 1.2 copy-done
  634.0 5.8 gather_fusion.5
  639.9 5.8 gather_fusion.4
  645.6 11.6 %pad_maximum_fusion = f32[3,2,256,2048]{3,2,1,0:T(8,128)} fusion(f32[3,2,256,1024]{3,2,1,0:T(8,128)} %gather_fusion.5, f32[3,2,256,1024]{3,2,1,0:T(8,128)} %gather_fusion.4), kind=kLoop, calls=%fused_computation.11 | loop fusion | flops 3145728 | bytes 25165824
  657.2 53.2 %gather.30 = f32[3,2,16,16,128,16]{5,4,3,2,1,0:T(8,128)} reshape(f32[3,2,256,2048]{3,2,1,0:T(8,128)} %pad_maximum_fusion) | data formatting | bytes 25165824 | tf_op jit(solution)/shard_map/jit(_take)/gather | solution.py:93
  710.4 64.7 %broadcast_select_fusion = f32[3,2,16,16,128,16]{5,4,3,2,1,0:T(8,128)} fusion(f32[3,2,16,16,128,16]{5,4,3,2,1,0:T(8,128)} %gather.30, pred[3]{0:T(512)(128)(4,1)S(1)} %compare_and_fusion), kind=kLoop, calls=%fused_computation.6 | loop fusion | flops 3145728 | bytes 25165828 | tf_op jit(solution)/shard_map/jit(_take)/select_n | solution.py:93
  775.1 11.1 %gather_fusion.2 = f32[6,2,16,128,16]{4,3,2,1,0:T(8,128)} fusion(f32[3,2,16,16,128,16]{5,4,3,2,1,0:T(8,128)} %broadcast_select_fusion, s32[6]{0:T(128)S(1)} %reshape.189), kind=kCustom, calls=%fused_computation.2 | custom fusion | bytes 3145776 | tf_op jit(solution)/shard_map/vmap(jit(_take))/gather | solution.py:38
  786.2 7.6 copy.89
  793.9 0.3 select_bitcast_fusion
  794.2 0.6 gather_fusion.3
  794.8 6.6 copy.90
  801.4 10.0 %gather.33 = f32[3,2,32,256]{3,2,1,0:T(8,128)S(1)} reshape(f32[3,2,16,2,128,2]{5,4,3,2,1,0:T(8,128)} %copy.90) | data formatting | bytes 393216 | tf_op jit(solution)/shard_map/vmap(jit(_take))/gather | solution.py:39
  811.3 0.7 broadcast_select_fusion.1
  812.1 0.0 all-gather.17.cloned.1.call-start
  812.1 69.7 %all-gather.13.cloned.1.call-done = f32[3,2,512,256]{3,2,1,0:T(8,128)} async-done(((f32[3,2,32,256]{3,2,1,0:T(8,128)}), f32[3,2,512,256]{3,2,1,0:T(8,128)}) %all-gather.13.cloned.1.call-update) | async-done | bytes 3145744 | tf_op jit(solution)/shard_map/all_gather | solution.py:54
  881.8 7.2 fusion.24
  889.0 0.1 fusion.34
  889.1 0.1 fusion.36
  889.2 1.3 maximum_subtract_fusion.2
  890.6 8.6 copy.98
  899.2 2.0 copy.97
  901.2 0.4 all-gather.17.cloned.1.call-done
  901.6 45.8 %fusion.4 = f32[3,2,2,256,2048]{4,3,2,1,0:T(8,128)} fusion(f32[3,2,512,2048]{3,2,1,0:T(8,128)} %all-gather.15.cloned.1.call-done, f32[3,2,256,512]{2,3,0,1:T(8,128)} %all-gather.17.cloned.1.call-done), kind=kOutput, calls=%fused_computation.13 | convolution fusion | flops 38654705664 | bytes 53477376 | tf_op jit(solution)/shard_map/bimk,bjkn->bijmn/dot_general | solution.py:19
  947.5 5.9 fusion.10
  953.4 5.9 fusion.12
  959.3 10.9 %maximum_subtract_fusion = f32[3,2,256,2048]{3,2,0,1:T(8,128)} fusion(f32[3,1,256,2048]{3,2,0,1:T(8,128)S(1)} %fusion.10, f32[3,1,256,2048]{3,2,0,1:T(8,128)S(1)} %fusion.12, f32[3,2,256,2048]{3,2,1,0:T(8,128)} %param.15), kind=kLoop, calls=%fused_computation.12 | loop fusion | flops 6291456 | bytes 37748736 | tf_op jit(solution)/shard_map/sub | solution.py:59
  970.2 11.7 %copy.100 = f32[3,2,256,2048]{3,2,1,0:T(8,128)} copy(f32[3,2,256,2048]{3,2,0,1:T(8,128)} %maximum_subtract_fusion) | data formatting | bytes 25165824
  981.9 2.4 copy.99
  (32 shorter events, 0.3 us)
Async XLA Ops:
  7.2 197.8 %all-gather.9.cloned.1.call-start = ((), (), s32[]{:S(2)}) async-start(), calls=%async_computation.1 | async-start | bytes 17825792 | tf_op jit(solution)/shard_map/all_gather | solution.py:46
  7.9 468.9 %all-gather.15.cloned.1.call-start = ((), (), s32[]{:S(2)}) async-start(), calls=%async_computation.4 | async-start | bytes 26738688 | tf_op jit(solution)/shard_map/all_gather | solution.py:46
  8.6 530.6 %all-gather.7.cloned.1.call-start = ((), (), s32[]{:S(2)}) async-start(), calls=%async_computation | async-start | bytes 2228224 | tf_op jit(solution)/shard_map/all_gather | solution.py:54
  19.5 5.6 copy-start.5
  39.0 532.2 %all-reduce.3.cloned.1.call-start = ((), (), s32[]{:S(2)}) async-start(), calls=%async_computation.6 | async-start | bytes 10485760 | tf_op jit(solution)/shard_map/psum | solution.py:15
  480.7 109.3 %all-gather.11.cloned.1.call-start = ((), (), s32[]{:S(2)}) async-start(), calls=%async_computation.2 | async-start | bytes 3145728 | tf_op jit(solution)/shard_map/all_gather | solution.py:56
  571.2 7.5 copy-start.6
  571.2 8.6 copy-start.7
  578.2 303.6 %all-gather.13.cloned.1.call-start = ((), (), s32[]{:S(2)}) async-start(), calls=%async_computation.3 | async-start | bytes 3342336 | tf_op jit(solution)/shard_map/all_gather | solution.py:54
  628.3 5.7 copy-start
  801.4 10.0 %copy-start.4 = (pred[3,256]{1,0:T(4,128)(4,1)S(1)}, pred[3,256]{1,0:T(4,128)(4,1)}, u32[]{:S(2)}) copy-start(pred[3,256]{1,0:T(4,128)(4,1)} %broadcast_in_dim.94) | copy-start | bytes 2308
  801.4 80.4 %copy-start.3 = (f32[3,2,512,256]{3,2,1,0:T(8,128)S(1)}, f32[3,2,512,256]{3,2,1,0:T(8,128)}, u32[]{:S(2)}) copy-start(f32[3,2,512,256]{3,2,1,0:T(8,128)} %get-tuple-element.21) | copy-start | bytes 9437188
  812.1 89.6 %all-gather.17.cloned.1.call-start = ((), (), s32[]{:S(2)}) async-start(), calls=%async_computation.5 | async-start | bytes 4718592 | tf_op jit(solution)/shard_map/all_gather | solution.py:56
  890.5 8.6 copy-start.2
  970.2 11.7 %copy-start.1 = (f32[3,2,256,512]{2,3,0,1:T(8,128)S(1)}, f32[3,2,256,512]{2,3,0,1:T(8,128)}, u32[]{:S(2)}) copy-start(f32[3,2,256,512]{2,3,0,1:T(8,128)} %all-gather.17.cloned.1.call-done) | copy-start | bytes 9437188
Sparse Core Ops, SparseCore 0:
  10.8 194.1 all-gather.8
  207.7 269.0 all-gather.14
  480.1 59.0 all-gather.6
  542.2 28.9 all-reduce.2
  578.3 11.7 all-gather.10
  812.2 69.5 all-gather.12
  890.7 10.9 all-gather.16
where the time goes:
time: 999 us; the launch traced here: 991 us
  waiting for transfers between devices  607 us (61%)
  local copies, waits for them, and re-layouts  162 us (16%)
  other arithmetic  116 us (12%)
  matrix products  91.1 us (9%)
  between operations  14.6 us (1%)
    all_gather x2, waiting for transfers between devices, supernode_level(): gathered_factor = lax.all_gather(factor_rows, 'row', axis=2, tiled=True)  435 us
    all_gather x2, waiting for transfers between devices, supernode_level(): lax.all_gather(chosen, 'row', axis=2, tiled=True)  128 us
    dot_general x4, matrix products, complex_product(): jnp.einsum(pattern, first_side, second_side, precision=lax.Precision.HIGH...  91.1 us
    gather x4, local copies, waits for them, and re-layouts, shards(): source = jnp.take(upper_blocks, parents_lower, axis=0)  69.4 us
    select_n x2, other arithmetic, shards(): source = jnp.take(upper_blocks, parents_lower, axis=0)  64.7 us
    psum x1, waiting for transfers between devices, from_root(): return lax.psum(block, axis)  32 us
    gather x6, local copies, waits for them, and re-layouts, pick_single(): matrix = jnp.take(matrix, chosen, axis=4)  29.3 us
    unnamed x20, local copies, waits for them, and re-layouts  25.9 us
  transfers between devices with their start and end apart: 7, of which 7 were waited for; matrix products, arithmetic and copies ran while one was open for 5% of the time, Pallas kernels for 0%

commit v1 on v0

--- a/solution.py
+++ b/solution.py
@@ -12,7 +12,7 @@
 
 def from_root(block, axis, source):
     block = jnp.where(lax.axis_index(axis) == source, block, jnp.zeros_like(block))
-    return lax.psum(block, axis)
+    return jnp.sum(lax.all_gather(block, axis), axis=0)
 
 
 def complex_product(first_side, second_side, pattern):

time: 999 us -> 881 us (0.88)
  waiting for transfers between devices: 607 us -> 480 us
  other arithmetic: 116 us -> 126 us
    all_gather x2, waiting for transfers between devices: 435 us -> 350 us  [supernode_level(): gathered_factor = lax.all_gather(factor_rows, 'row', axis=2, tiled=True)]
    psum x1 -> x0, waiting for transfers between devices: 32 us -> none  [from_root(): return lax.psum(block, axis)]
  transfers between devices with their start and end apart: 7 -> 8, of which waited for: 7 -> 6; matrix products, arithmetic and copies ran while one was open for 5% -> 31% of each run, Pallas kernels for 0% -> 0%
where the time goes in v1:
time: 881 us; the launch traced here: 872 us
  waiting for transfers between devices  480 us (54%)
  local copies, waits for them, and re-layouts  160 us (18%)
  other arithmetic  126 us (14%)
  matrix products  90.4 us (10%)
  between operations  14.9 us (2%)
    all_gather x2, waiting for transfers between devices, supernode_level(): gathered_factor = lax.all_gather(factor_rows, 'row', axis=2, tiled=True)  350 us
    all_gather x2, waiting for transfers between devices, supernode_level(): lax.all_gather(chosen, 'row', axis=2, tiled=True)  121 us
    dot_general x4, matrix products, complex_product(): jnp.einsum(pattern, first_side, second_side, precision=lax.Precision.HIGH...  90.4 us
    gather x4, local copies, waits for them, and re-layouts, shards(): source = jnp.take(upper_blocks, parents_lower, axis=0)  69.4 us
    select_n x2, other arithmetic, shards(): source = jnp.take(upper_blocks, parents_lower, axis=0)  66.4 us
    gather x6, local copies, waits for them, and re-layouts, pick_single(): matrix = jnp.take(matrix, chosen, axis=4)  29.1 us
    unnamed x20, local copies, waits for them, and re-layouts  26 us
    gather x6, local copies, waits for them, and re-layouts, pick_single(): matrix = jnp.take(matrix, chosen, axis=2)  19.5 us
  transfers between devices with their start and end apart: 8, of which 6 were waited for; matrix products, arithmetic and copies ran while one was open for 31% of the time, Pallas kernels for 0%

profile of v1, /device:TPU:0, one launch (start us, length us, event | category | flops | bytes accessed | tf_op | source)
XLA Modules:
  0.0 872.3 jit_solution(3422598973099315887)
XLA Ops:
  7.2 0.7 all-gather.13.cloned.1.call-update
  8.0 197.0 %all-gather.13.cloned.1.call-done = f32[2,2,512,2048]{3,2,1,0:T(8,128)} async-done(((f32[2,2,32,2048]{3,2,1,0:T(8,128)}), f32[2,2,512,2048]{3,2,1,0:T(8,128)}) %all-gather.13.cloned.1.call-update) | async-done | bytes 16777232 | tf_op jit(solution)/shard_map/all_gather | solution.py:46
  205.0 3.1 dynamic-slice_select_fusion.1
  208.1 0.1 reshape.177
  208.2 10.0 %broadcast_in_dim.86 = f32[2,16,4,128,4]{4,3,2,1,0:T(8,128)} reshape(f32[2,64,512]{2,1,0:T(8,128)S(1)} %copy-done.3) | data formatting | bytes 524288 | tf_op jit(solution)/shard_map/broadcast_in_dim | solution.py:86
  218.2 5.2 copy.101
  223.4 0.1 broadcast_in_dim.87
  223.5 0.6 gather_fusion
  224.1 0.1 fusion.40
  224.2 0.6 gather_fusion.1
  224.7 4.6 copy.103
  229.4 6.9 gather.28
  236.3 0.1 broadcast_in_dim.83
  236.5 0.7 broadcast_select_fusion.2
  237.2 0.0 all-gather.15.cloned.1.call-start
  237.3 2.8 reduce_sum.18
  240.0 57.0 %all-gather.11.cloned.1.call-done = f32[2,2,512,256]{3,2,1,0:T(8,128)} async-done(((f32[2,2,32,256]{3,2,1,0:T(8,128)}), f32[2,2,512,256]{3,2,1,0:T(8,128)}) %all-gather.11.cloned.1.call-update) | async-done | bytes 2097168 | tf_op jit(solution)/shard_map/all_gather | solution.py:54
  297.0 5.1 fusion.29
  302.1 0.1 fusion.37
  302.2 0.1 fusion.39
  302.2 1.1 maximum_subtract_fusion.3
  303.4 0.5 all-gather.19.cloned.1.call-update
  303.9 0.5 all-gather.25.cloned.1.call-start
  304.5 0.1 copy.112
  304.6 0.1 reshape.189
  304.6 0.1 copy.110
  304.8 0.7 broadcast_in_dim.94
  305.5 7.3 all-gather.15.cloned.1.call-done
  312.8 32.2 %fusion.7 = f32[2,2,2,256,2048]{4,3,2,1,0:T(8,128)S(1)} fusion(f32[2,2,512,2048]{3,2,1,0:T(8,128)} %all-gather.13.cloned.1.call-done, f32[2,2,256,512]{2,3,0,1:T(8,128)} %all-gather.15.cloned.1.call-done), kind=kOutput, calls=%fused_computation.15 | convolution fusion | flops 25769803776 | bytes 35651584 | tf_op jit(solution)/shard_map/bimk,bjkn->bijmn/dot_general | solution.py:19
  345.1 0.8 fusion.13
  345.9 0.8 fusion.15
  346.6 4.5 maximum_subtract_fusion.1
  351.1 4.5 fusion.41
  355.7 1.3 copy-done
  356.9 5.8 gather_fusion.4
  362.7 5.8 gather_fusion.5
  368.6 12.8 %pad_maximum_fusion = f32[3,2,256,2048]{3,2,1,0:T(8,128)} fusion(f32[3,2,256,1024]{3,2,1,0:T(8,128)} %gather_fusion.5, f32[3,2,256,1024]{3,2,1,0:T(8,128)} %gather_fusion.4), kind=kLoop, calls=%fused_computation.11 | loop fusion | flops 3145728 | bytes 25165824
  381.3 53.3 %gather.30 = f32[3,2,16,16,128,16]{5,4,3,2,1,0:T(8,128)} reshape(f32[3,2,256,2048]{3,2,1,0:T(8,128)} %pad_maximum_fusion) | data formatting | bytes 25165824 | tf_op jit(solution)/shard_map/jit(_take)/gather | solution.py:93
  434.6 152.9 %all-gather.19.cloned.1.call-done = f32[3,2,512,2048]{3,2,1,0:T(8,128)} async-done(((f32[3,2,32,2048]{3,2,1,0:T(8,128)}), f32[3,2,512,2048]{3,2,1,0:T(8,128)}) %all-gather.19.cloned.1.call-update) | async-done | bytes 25165840 | tf_op jit(solution)/shard_map/all_gather | solution.py:46
  587.5 3.9 dynamic-slice_select_fusion
  591.5 66.4 %broadcast_select_fusion = f32[3,2,16,16,128,16]{5,4,3,2,1,0:T(8,128)} fusion(f32[3,2,16,16,128,16]{5,4,3,2,1,0:T(8,128)} %gather.30, pred[3]{0:T(512)(128)(4,1)S(1)} %compare_and_fusion), kind=kLoop, calls=%fused_computation.6 | loop fusion | flops 3145728 | bytes 25165828 | tf_op jit(solution)/shard_map/jit(_take)/select_n | solution.py:93
  657.9 11.1 %gather_fusion.2 = f32[6,2,16,128,16]{4,3,2,1,0:T(8,128)} fusion(f32[3,2,16,16,128,16]{5,4,3,2,1,0:T(8,128)} %broadcast_select_fusion, s32[6]{0:T(128)S(1)} %reshape.189), kind=kCustom, calls=%fused_computation.2 | custom fusion | bytes 3145776 | tf_op jit(solution)/shard_map/vmap(jit(_take))/gather | solution.py:38
  669.0 7.6 copy.114
  676.6 0.3 select_bitcast_fusion
  676.9 0.6 gather_fusion.3
  677.5 6.6 copy.115
  684.1 9.8 %gather.33 = f32[3,2,32,256]{3,2,1,0:T(8,128)S(1)} reshape(f32[3,2,16,2,128,2]{5,4,3,2,1,0:T(8,128)} %copy.115) | data formatting | bytes 393216 | tf_op jit(solution)/shard_map/vmap(jit(_take))/gather | solution.py:39
  693.9 0.7 broadcast_select_fusion.1
  694.7 0.3 all-gather.21.cloned.1.call-start
  695.0 3.6 reduce_sum.19
  698.6 64.0 %all-gather.17.cloned.1.call-done = f32[3,2,512,256]{3,2,1,0:T(8,128)} async-done(((f32[3,2,32,256]{3,2,1,0:T(8,128)}), f32[3,2,512,256]{3,2,1,0:T(8,128)}) %all-gather.17.cloned.1.call-update) | async-done | bytes 3145744 | tf_op jit(solution)/shard_map/all_gather | solution.py:54
  762.6 7.2 fusion.24
  769.8 0.1 fusion.34
  769.9 0.1 fusion.36
  770.0 1.3 maximum_subtract_fusion.2
  771.3 8.6 copy.123
  780.0 2.0 copy.122
  782.0 0.4 all-gather.21.cloned.1.call-done
  782.4 45.9 %fusion.4 = f32[3,2,2,256,2048]{4,3,2,1,0:T(8,128)} fusion(f32[3,2,512,2048]{3,2,1,0:T(8,128)} %all-gather.19.cloned.1.call-done, f32[3,2,256,512]{2,3,0,1:T(8,128)} %all-gather.21.cloned.1.call-done), kind=kOutput, calls=%fused_computation.13 | convolution fusion | flops 38654705664 | bytes 53477376 | tf_op jit(solution)/shard_map/bimk,bjkn->bijmn/dot_general | solution.py:19
  828.3 5.9 fusion.10
  834.2 5.9 fusion.12
  840.1 10.9 %maximum_subtract_fusion = f32[3,2,256,2048]{3,2,0,1:T(8,128)} fusion(f32[3,1,256,2048]{3,2,0,1:T(8,128)S(1)} %fusion.10, f32[3,1,256,2048]{3,2,0,1:T(8,128)S(1)} %fusion.12, f32[3,2,256,2048]{3,2,1,0:T(8,128)} %param.15), kind=kLoop, calls=%fused_computation.12 | loop fusion | flops 6291456 | bytes 37748736 | tf_op jit(solution)/shard_map/sub | solution.py:59
  851.0 11.7 %copy.125 = f32[3,2,256,2048]{3,2,1,0:T(8,128)} copy(f32[3,2,256,2048]{3,2,0,1:T(8,128)} %maximum_subtract_fusion) | data formatting | bytes 25165824
  862.7 2.4 copy.124
  (37 shorter events, 0.5 us)
Async XLA Ops:
  7.2 201.0 %copy-start.5 = (s32[2,2]{1,0:T(2,128)S(1)}, s32[2,2]{1,0:T(2,128)}, u32[]{:S(2)}) copy-start(s32[2,2]{1,0:T(2,128)} %param.9) | copy-start | bytes 52
  7.2 201.1 %copy-start.3 = (f32[2,64,512]{2,1,0:T(8,128)S(1)}, f32[2,64,512]{2,1,0:T(8,128)}, u32[]{:S(2)}) copy-start(f32[2,64,512]{2,1,0:T(8,128)} %param.8) | copy-start | bytes 786436
  7.2 197.8 %all-gather.13.cloned.1.call-start = ((), (), s32[]{:S(2)}) async-start(), calls=%async_computation.1 | async-start | bytes 17825792 | tf_op jit(solution)/shard_map/all_gather | solution.py:46
  7.9 229.3 %all-gather.23.cloned.1.call-start = ((), (), s32[]{:S(2)}) async-start(), calls=%async_computation.6 | async-start | bytes 6291456 | tf_op jit(solution)/shard_map/all_gather | solution.py:15
  208.1 88.9 %all-gather.11.cloned.1.call-start = ((), (), s32[]{:S(2)}) async-start(), calls=%async_computation | async-start | bytes 2228224 | tf_op jit(solution)/shard_map/all_gather | solution.py:54
  237.2 75.7 %all-gather.15.cloned.1.call-start = ((), (), s32[]{:S(2)}) async-start(), calls=%async_computation.2 | async-start | bytes 3145728 | tf_op jit(solution)/shard_map/all_gather | solution.py:56
  240.0 64.4 %copy-start.6 = (s32[3,2]{0,1:T(2,128)S(1)}, s32[3,2]{0,1:T(2,128)}, u32[]{:S(2)}) copy-start(s32[3,2]{0,1:T(2,128)} %param.13) | copy-start | bytes 76
  240.0 65.5 %copy-start.7 = (s32[3]{0:T(128)S(1)}, s32[3]{0:T(128)}, u32[]{:S(2)}) copy-start(s32[3]{0:T(128)} %param.12) | copy-start | bytes 40
  303.3 284.2 %all-gather.19.cloned.1.call-start = ((), (), s32[]{:S(2)}) async-start(), calls=%async_computation.4 | async-start | bytes 26738688 | tf_op jit(solution)/shard_map/all_gather | solution.py:46
  303.9 391.0 %all-gather.25.cloned.1.call-start = ((), (), s32[]{:S(2)}) async-start(), calls=%async_computation.7 | async-start | bytes 9437184 | tf_op jit(solution)/shard_map/all_gather | solution.py:15
  351.1 5.8 copy-start
  591.4 171.1 %all-gather.17.cloned.1.call-start = ((), (), s32[]{:S(2)}) async-start(), calls=%async_computation.3 | async-start | bytes 3342336 | tf_op jit(solution)/shard_map/all_gather | solution.py:54
  684.1 9.8 %copy-start.4 = (pred[3,256]{1,0:T(4,128)(4,1)S(1)}, pred[3,256]{1,0:T(4,128)(4,1)}, u32[]{:S(2)}) copy-start(pred[3,256]{1,0:T(4,128)(4,1)} %broadcast_in_dim.94) | copy-start | bytes 2308
  694.7 87.7 %all-gather.21.cloned.1.call-start = ((), (), s32[]{:S(2)}) async-start(), calls=%async_computation.5 | async-start | bytes 4718592 | tf_op jit(solution)/shard_map/all_gather | solution.py:56
  771.3 8.6 copy-start.2
  851.0 11.7 %copy-start.1 = (f32[3,2,256,512]{2,3,0,1:T(8,128)S(1)}, f32[3,2,256,512]{2,3,0,1:T(8,128)}, u32[]{:S(2)}) copy-start(f32[3,2,256,512]{2,3,0,1:T(8,128)} %all-gather.21.cloned.1.call-done) | copy-start | bytes 9437188
Sparse Core Ops, SparseCore 0:
  10.8 194.1 all-gather.12
  208.2 11.8 all-gather.22
  237.3 59.6 all-gather.10
  303.5 9.3 all-gather.14
  315.4 272.0 all-gather.18
  591.5 14.9 all-gather.24
  694.8 67.7 all-gather.16
  771.4 10.9 all-gather.20
